TPU v7x, 128 devices: a whole 4x4x4 slice. The times are simulated.
128 devices in a mesh: dp: 2 (over core), context: 16 (over y, x), tensor: 4 (over z).
Axes of the slice: x: 4, y: 4, z: 4, core: 2. Of those that a mesh axis runs over, the one named last changes fastest.
Arguments:
- ids: int32 [16384], P(('dp', 'context', 'tensor')), parts along dimension 0, may hold values from 65 to 84, as said below
- block_order: int32 [64], P('dp'), parts along dimension 0, may hold values from 0 to 31, each once
- embed: bfloat16 [512, 4096], replicated, may hold values from -6 to 6
- mix_gain: float32 [4096], replicated, may hold values from 0.5 to 2
- in_proj: bfloat16 [3, 4096, 2048], P(None, None, 'tensor'), may hold values from -0.09375 to 0.09375
- short_filter: float32 [3, 3, 2048], P(None, None, 'tensor'), may hold values from -1 to 1
- long_filter: float32 [128, 128], P('tensor'), as said below
- conv_skip: float32 [2048], P('tensor'), may hold values from -1 to 1
- hyena_out: bfloat16 [2048, 4096], P('tensor'), may hold values from -0.125 to 0.125
- attn_gain: float32 [4096], replicated, may hold values from 0.5 to 2
- qkv_proj: bfloat16 [3, 4096, 2048], P(None, None, 'tensor'), as said below
- attn_out: bfloat16 [2048, 4096], P('tensor'), may hold values from -0.5 to 0.5
Outputs:
- stream_out: float32 [16384, 4096], P(('dp', 'context', 'tensor')), parts along dimension 0
There are 2 independent parts, one for each index of `dp`. A program takes and returns all parts, laid end to end along the dimension named above; an argument that names none is the same for every part. Nothing has to cross between parts.
Inputs may be any that keep to these rules, and one draw needn't show every extreme that they name: `ids`: every id is the code of a base: 65, 67, 71 or 84. `block_order`: every block lies in exactly one slot. `long_filter`: real-valued filter taps. `qkv_proj`: real-valued projection weights.
All inputs are finite; a program needn't handle non-finite values.
Results may differ from a plain program's by a relative error of at most 0.01.
Values may be sent and summed in bfloat16 or wider, within the bound.
A program may use at most 192 MiB of HBM per device.

v0:
```python
import math
import jax
import jax.numpy as jnp
from jax import lax
from jax.sharding import PartitionSpec as P

HD = 128
GROUP_CH = 16
EPS = 1e-06
THETA = 1000000.0
NEG_FILL = -1e30


def rms_scale(row_data, gain_vec):
    values = row_data.astype(jnp.float32)
    factor = lax.rsqrt(jnp.mean(values * values, axis=-1, keepdims=True) + EPS)
    return (values * factor * gain_vec).astype(jnp.bfloat16)


def toeplitz(long_filter):
    filter_len = long_filter.shape[1]
    tap_lag = (
        jnp.arange(filter_len, dtype=jnp.int32)[:, None]
        - jnp.arange(filter_len, dtype=jnp.int32)[None, :]
    )
    near_taps = jnp.take(long_filter, jnp.clip(tap_lag, 0, filter_len - 1), axis=1)
    far_taps = jnp.take(long_filter, jnp.clip(tap_lag + filter_len, 0, filter_len - 1), axis=1)
    near_taps = jnp.where(tap_lag[None] >= 0, near_taps, jnp.zeros_like(near_taps))
    far_taps = jnp.where(tap_lag[None] < 0, far_taps, jnp.zeros_like(far_taps))
    return (near_taps, far_taps)


def long_conv(padded, long_filter, group_width):
    filter_len = long_filter.shape[1]
    near_taps, far_taps = toeplitz(long_filter)
    row_total = padded.shape[0]
    chan_total = padded.shape[1]
    blocks = padded.reshape(
        row_total // filter_len, filter_len, chan_total // group_width, group_width
    )
    current_part = jnp.einsum(
        "grs,bsgc->brgc", near_taps, blocks[1:], precision=lax.Precision.HIGHEST
    )
    before = jnp.einsum("grs,bsgc->brgc", far_taps, blocks[:-1], precision=lax.Precision.HIGHEST)
    return (current_part + before).reshape(row_total - filter_len, chan_total)


def short_conv(padded_rows, short_filter, out_len):
    taps = short_filter.shape[1]
    result = jnp.zeros((padded_rows.shape[0], out_len, padded_rows.shape[2]), jnp.float32)
    for tap_at in range(taps):
        offset = taps - 1 - tap_at
        result = (
            result + short_filter[:, tap_at][:, None, :] * padded_rows[:, offset : offset + out_len]
        )
    return result


def rotate(values, positions, head_dim):
    half_dim = head_dim // 2
    inverse_freq = THETA ** (-(2.0 * jnp.arange(half_dim, dtype=jnp.float32)) / head_dim)
    angles = positions.astype(jnp.float32)[:, None] * inverse_freq[None, :]
    cosine_part = jnp.cos(angles)[:, None, :]
    sine_part = jnp.sin(angles)[:, None, :]
    lower_half = values[..., :half_dim]
    upper_half = values[..., half_dim:]
    return jnp.concatenate(
        [
            lower_half * cosine_part - upper_half * sine_part,
            upper_half * cosine_part + lower_half * sine_part,
        ],
        axis=-1,
    )


def body(
    ids,
    block_order,
    embed,
    mix_gain,
    in_proj,
    short_filter,
    long_filter,
    conv_skip,
    hyena_out,
    attn_gain,
    qkv_proj,
    attn_out,
):
    tok_rows = ids.shape[0]
    tensor_count = lax.axis_size("tensor")
    context_count = lax.axis_size("context")
    ctx_rows = tok_rows * tensor_count
    block_rows = ctx_rows // 2
    filter_len = long_filter.shape[1]
    short_len = short_filter.shape[1]
    halo_len = filter_len + short_len - 2
    chan_local = in_proj.shape[2]
    context_at = lax.axis_index("context")
    vocab_ids = jnp.arange(embed.shape[0], dtype=jnp.int32)
    chosen = (ids[:, None] == vocab_ids[None, :]).astype(jnp.bfloat16)
    embedded = jnp.dot(chosen, embed, preferred_element_type=jnp.float32).astype(jnp.bfloat16)
    embedded_all = lax.all_gather(embedded, "tensor", axis=0, tiled=True)
    mixed_in = rms_scale(embedded_all, mix_gain)
    projected = jnp.einsum(
        "rd,jdc->jrc", mixed_in, in_proj, preferred_element_type=jnp.float32
    ).astype(jnp.bfloat16)
    slot_ids = jnp.arange(2 * context_count, dtype=jnp.int32)
    slot_pair = 2 * context_at + jnp.arange(2, dtype=jnp.int32)
    owned_blocks = jnp.sum(
        jnp.where(slot_ids[None, :] == slot_pair[:, None], block_order[None, :], 0), axis=1
    )
    local_pos = (
        owned_blocks[:, None] * block_rows + jnp.arange(block_rows, dtype=jnp.int32)[None, :]
    ).reshape(ctx_rows)
    tail_rows = jnp.stack(
        [projected[:, block_rows - halo_len : block_rows], projected[:, ctx_rows - halo_len :]]
    )
    all_tails = lax.all_gather(tail_rows, "context", axis=0, tiled=True)
    out_len = filter_len - 1 + block_rows
    pieces = []
    for block_at in range(2):
        holder_hit = (block_order == owned_blocks[block_at] - 1).astype(jnp.bfloat16)
        before_rows = jnp.einsum(
            "s,sjrc->jrc", holder_hit, all_tails, preferred_element_type=jnp.float32
        )
        own_rows = projected[:, block_at * block_rows : (block_at + 1) * block_rows].astype(
            jnp.float32
        )
        extended = jnp.concatenate([before_rows, own_rows], axis=1)
        filtered = short_conv(extended, short_filter, out_len)
        gated_rows = filtered[1] * filtered[2]
        padded = jnp.concatenate([jnp.zeros((1, chan_local), jnp.float32), gated_rows], axis=0)
        long_mix = long_conv(padded, long_filter, GROUP_CH)
        own_gate = gated_rows[filter_len - 1 :]
        pieces.append(
            (filtered[0, filter_len - 1 :] * (long_mix + conv_skip * own_gate)).astype(jnp.bfloat16)
        )
    hyena_mix = jnp.concatenate(pieces, axis=0)
    hyena_own = lax.psum_scatter(
        jnp.dot(hyena_mix, hyena_out, preferred_element_type=jnp.float32),
        "tensor",
        scatter_dimension=0,
        tiled=True,
    )
    stream_own = embedded.astype(jnp.float32) + hyena_own
    stream_all = lax.all_gather(stream_own, "tensor", axis=0, tiled=True)
    attn_in = rms_scale(stream_all, attn_gain)
    projections = jnp.einsum("rd,jdf->jrf", attn_in, qkv_proj, preferred_element_type=jnp.float32)
    local_heads = projections.shape[2] // HD
    shaped = projections.reshape(3, ctx_rows, local_heads, HD)
    queries = rotate(shaped[0], local_pos, HD).astype(jnp.bfloat16)
    keys_flat = (
        rotate(shaped[1], local_pos, HD).astype(jnp.bfloat16).reshape(ctx_rows, local_heads * HD)
    )
    values_flat = shaped[2].astype(jnp.bfloat16).reshape(ctx_rows, local_heads * HD)
    score_scale = HD ** (-0.5)
    start_state = (
        jnp.full((2, block_rows, local_heads), NEG_FILL, jnp.float32),
        jnp.zeros((2, block_rows, local_heads), jnp.float32),
        jnp.zeros((2, block_rows, local_heads, HD), jnp.float32),
    )
    key_piece = lax.all_gather(keys_flat, "context", axis=0, tiled=True)
    value_piece = lax.all_gather(values_flat, "context", axis=0, tiled=True)
    piece_len = key_piece.shape[0]
    sub_len = math.gcd(piece_len, 512)

    def attend_sub(sub_index, carried):
        key_block = lax.dynamic_slice_in_dim(key_piece, sub_index * sub_len, sub_len, 0).reshape(
            sub_len, local_heads, HD
        )
        value_block = lax.dynamic_slice_in_dim(
            value_piece, sub_index * sub_len, sub_len, 0
        ).reshape(sub_len, local_heads, HD)
        row_ids = sub_index * sub_len + jnp.arange(sub_len, dtype=jnp.int32)
        holder = row_ids // block_rows
        key_pos = (
            jnp.sum(
                jnp.where(holder[:, None] == slot_ids[None, :], block_order[None, :], 0), axis=1
            )
            * block_rows
            + row_ids % block_rows
        )
        top_all, sums_all, weighted_all = carried
        outputs = []
        for block_at in range(2):
            query_rows = queries[block_at * block_rows : (block_at + 1) * block_rows]
            query_pos = local_pos[block_at * block_rows : (block_at + 1) * block_rows]
            top_score = top_all[block_at]
            weight_sum = sums_all[block_at]
            weighted = weighted_all[block_at]
            scores = (
                jnp.einsum(
                    "qhd,khd->qhk", query_rows, key_block, preferred_element_type=jnp.float32
                )
                * score_scale
            )
            visible = key_pos[None, None, :] <= query_pos[:, None, None]
            scores = jnp.where(visible, scores, NEG_FILL)
            new_top = jnp.maximum(top_score, jnp.max(scores, axis=-1))
            rescale = jnp.exp(top_score - new_top)
            weights = jnp.where(visible, jnp.exp(scores - new_top[..., None]), 0.0)
            weight_sum = weight_sum * rescale + jnp.sum(weights, axis=-1)
            weighted = weighted * rescale[..., None] + jnp.einsum(
                "qhk,khd->qhd",
                weights.astype(jnp.bfloat16),
                value_block,
                preferred_element_type=jnp.float32,
            )
            result = (new_top, weight_sum, weighted)
            outputs.append(result)
        return tuple((jnp.stack([entry[field] for entry in outputs]) for field in range(3)))

    top_final, sums_final, weighted_final = lax.fori_loop(
        0, piece_len // sub_len, attend_sub, start_state
    )
    attended = (
        (weighted_final / sums_final[..., None])
        .astype(jnp.bfloat16)
        .reshape(ctx_rows, local_heads * HD)
    )
    attn_own = lax.psum_scatter(
        jnp.dot(attended, attn_out, preferred_element_type=jnp.float32).astype(jnp.bfloat16),
        "tensor",
        scatter_dimension=0,
        tiled=True,
    ).astype(jnp.float32)
    return stream_own + attn_own


def solution(mesh):
    placed = (
        P(("dp", "context", "tensor")),
        P("dp"),
        P(),
        P(),
        P(None, None, "tensor"),
        P(None, None, "tensor"),
        P("tensor", None),
        P("tensor"),
        P("tensor", None),
        P(),
        P(None, None, "tensor"),
        P("tensor", None),
    )
    return jax.shard_map(
        body,
        mesh=mesh,
        in_specs=placed,
        out_specs=P(("dp", "context", "tensor"), None),
        check_vma=False,
    )
```

profile of v0, /device:TPU:1, one launch (start us, length us, event | category | flops | bytes accessed | tf_op | source)
XLA Modules:
  0.0 769.6 jit_solution(17294564735795966699)
XLA Ops:
  6.5 3.9 convolution_convert_fusion.1
  10.5 51.8 %all-gather.7.cloned.1.call-done = bf16[512,4096]{1,0:T(8,128)(2,1)} async-done(((bf16[128,4096]{1,0:T(8,128)(2,1)}), bf16[512,4096]{1,0:T(8,128)(2,1)}) %all-gather.7.cloned.1.call-update) | async-done | bytes 4194320 | tf_op jit(solution)/shard_map/all_gather | solution.py:103
  65.8 9.9 %fusion.83 = bf16[3,512,512]{2,1,0:T(8,128)(2,1)S(1)} fusion(bf16[3,4096,512]{2,1,0:T(8,128)(2,1)} %param.20, bf16[512,4096]{1,0:T(8,128)(2,1)S(1)} %copy-done.10, f32[4096]{0:T(1024)S(1)} %copy-done.18, f32[512]{0:T(512)S(1)} %add_rsqrt_fusion.1), kind=kOutput, calls=%fused_computation.128 | convolution fusion | flops 6451625984 | bytes 18368512 | tf_op jit(solution)/shard_map/rd,jdc->jrc/dot_general | solution.py:105
  80.6 54.8 %gather_fusion.1 = f32[16384,32]{1,0:T(8,128)} fusion(f32[32,128]{0,1:T(8,128)S(1)} %copy.81, s32[16384]{0:T(1024)S(1)} %bitcast_clamp_fusion), kind=kCustom, calls=%fused_computation.1.clone | custom fusion | bytes 4259840 | tf_op jit(solution)/shard_map/jit(_take)/gather | solution.py:27
  135.4 6.5 copy.86
  141.9 54.8 %gather_fusion = f32[16384,32]{1,0:T(8,128)} fusion(f32[32,128]{0,1:T(8,128)S(1)} %copy.81, s32[16384]{0:T(1024)S(1)} %bitcast_clamp_fusion.1), kind=kCustom, calls=%fused_computation.clone | custom fusion | bytes 4259840 | tf_op jit(solution)/shard_map/jit(_take)/gather | solution.py:26
  196.7 5.5 copy.82
  202.3 3.4 slice_convert_fusion.2
  205.8 8.8 %fusion.38 = f32[1,3,129,512]{3,0,2,1:T(1,128)S(1)} fusion(bf16[32,3,129,512]{3,2,1,0:T(8,128)(2,1)} %all-gather.9.cloned.1.call-done, s32[32]{0:T(128)S(1)} %copy-done.14, s32[]{:T(128)} %bitcast.22), kind=kOutput, calls=%fused_computation.69 | convolution fusion | flops 12681248 | bytes 13473924 | tf_op jit(solution)/shard_map/s,sjrc->jrc/dot_general | solution.py:124
  214.6 3.7 fusion.40
  233.2 5.0 fusion.71
  238.2 3.4 fusion.89
  247.1 5.2 fusion.69
  257.3 4.6 fusion.95
  264.8 7.8 %fusion.120 = f32[512,4096]{1,0:T(8,128)} fusion(bf16[512,4096]{1,0:T(8,128)(2,1)} %param.24, bf16[256,512]{1,0:T(8,128)(2,1)S(1)} %get-tuple-element.361, bf16[256,512]{1,0:T(8,128)(2,1)S(1)} %get-tuple-element.360), kind=kOutput, calls=%fused_computation.170 | convolution fusion | flops 2148532224 | bytes 13107200 | tf_op jit(solution)/shard_map/dot_general | solution.py:141
  272.7 81.1 %reduce-scatter.3.cloned.1.call-done = f32[128,4096]{1,0:T(8,128)} async-done(((f32[512,4096]{1,0:T(8,128)}), f32[128,4096]{1,0:T(8,128)}) %reduce-scatter.3.cloned.1.call-update) | async-done | bytes 2097168 | tf_op jit(solution)/shard_map/reduce_scatter | solution.py:140
  357.6 82.3 %all-gather.11.cloned.1.call-done = f32[512,4096]{1,0:T(8,128)} async-done(((f32[128,4096]{1,0:T(8,128)}), f32[512,4096]{1,0:T(8,128)}) %all-gather.11.cloned.1.call-update) | async-done | bytes 8388624 | tf_op jit(solution)/shard_map/all_gather | solution.py:147
  439.9 4.2 multiply_reduce_fusion
  445.6 11.3 %fusion.77 = f32[3,512,512]{1,2,0:T(8,128)} fusion(bf16[3,4096,512]{2,1,0:T(8,128)(2,1)} %param.26, f32[512,4096]{1,0:T(8,128)S(1)} %copy-done.5, f32[4096]{0:T(1024)S(1)} %copy-done.19, f32[512]{0:T(512)S(1)} %add_rsqrt_fusion), kind=kOutput, calls=%fused_computation.126 | convolution fusion | flops 6448742400 | bytes 24135680 | tf_op jit(solution)/shard_map/rd,jdf->jrf/dot_general | solution.py:149
  462.5 75.8 %all-gather.13.cloned.1.call-done = bf16[8192,512]{0,1:T(8,128)(2,1)} async-done(((bf16[512,512]{0,1:T(8,128)(2,1)}), bf16[8192,512]{0,1:T(8,128)(2,1)}) %all-gather.13.cloned.1.call-update) | async-done | bytes 8388624 | tf_op jit(solution)/shard_map/all_gather | solution.py:163
  538.2 79.6 %all-gather.15.cloned.1.call-done = bf16[1,8192,512]{1,2,0:T(8,128)(2,1)} async-done(((bf16[1,512,512]{1,2,0:T(8,128)(2,1)}), bf16[1,8192,512]{1,2,0:T(8,128)(2,1)}) %all-gather.15.cloned.1.call-update) | async-done | bytes 8388624 | tf_op jit(solution)/shard_map/all_gather | solution.py:164
  618.0 87.3 %while.20 = (s32[]{:T(128)}, f32[2,256,4]{1,2,0:T(4,128)S(1)}, f32[2,256,4]{1,2,0:T(4,128)S(1)}, f32[2,256,4,128]{1,3,2,0:T(8,128)S(1)}, s32[32]{0:T(128)S(1)}, ...) while((s32[]{:T(128)}, f32[2,256,4]{1,2,0:T(4,128)S(1)}, ...), condition=%wide.region_10.12_spmd.clone, body=%wide.region_4.11_spmd.clone.sunk | while | flops 551627264 | bytes 22718784 | solution.py:214
  705.6 6.5 convolution_convert_fusion
  712.2 47.6 %reduce-scatter.5.cloned.1.call-done = bf16[128,4096]{1,0:T(8,128)(2,1)} async-done(((bf16[512,4096]{1,0:T(8,128)(2,1)}), bf16[128,4096]{1,0:T(8,128)(2,1)}) %reduce-scatter.5.cloned.1.call-update) | async-done | bytes 1048592 | tf_op jit(solution)/shard_map/reduce_scatter | solution.py:222
  (387 shorter events, 134.9 us)
Async XLA Ops:
  6.5 55.8 %all-gather.7.cloned.1.call-start = ((), (), s32[]{:S(2)}) async-start(), calls=%async_computation.2 | async-start | bytes 5242880 | tf_op jit(solution)/shard_map/all_gather | solution.py:103
  10.5 55.1 %copy-start.18 = (f32[4096]{0:T(1024)S(1)}, f32[4096]{0:T(1024)}, u32[]{:S(2)}) copy-start(f32[4096]{0:T(1024)} %param.19) | copy-start | bytes 49156
  10.5 195.3 %all-gather.9.cloned.1.call-start = ((), (), s32[]{:S(2)}) async-start(), calls=%async_computation.3 | async-start | bytes 14204928 | tf_op jit(solution)/shard_map/all_gather | solution.py:119
  62.3 3.4 copy-start.10
  76.8 1.6 copy-start.14
  76.8 3.6 copy-start.16
  76.9 3.6 copy-start.15
  78.1 275.6 %reduce-scatter.3.cloned.1.call-start = ((), (), s32[]{:S(2)}) async-start(), calls=%async_computation.4 | async-start | bytes 10485760 | tf_op jit(solution)/shard_map/reduce_scatter | solution.py:140
  205.8 8.8 %copy-start = (bf16[32,3,129,512]{3,2,1,0:T(8,128)(2,1)S(1)}, bf16[32,3,129,512]{3,2,1,0:T(8,128)(2,1)}, u32[]{:S(2)}) copy-start(bf16[32,3,129,512]{3,2,1,0:T(8,128)(2,1)} %all-gather.9.cloned.1.call-done) | copy-start | bytes 38043652
  218.3 1.4 copy-start.6
  218.3 1.9 copy-start.7
  222.3 1.4 copy-start.2
  222.3 2.4 copy-start.3
  233.2 5.0 copy-start.13
  247.1 5.2 copy-start.8
  261.9 1.3 copy-start.12
  272.6 81.2 %copy-start.4 = (bf16[128,4096]{1,0:T(8,128)(2,1)S(1)}, bf16[128,4096]{1,0:T(8,128)(2,1)}, u32[]{:S(2)}) copy-start(bf16[128,4096]{1,0:T(8,128)(2,1)} %convolution_convert_fusion.1) | copy-start | bytes 3145732
  272.6 167.3 %all-gather.11.cloned.1.call-start = ((), (), s32[]{:S(2)}) async-start(), calls=%async_computation.5 | async-start | bytes 10485760 | tf_op jit(solution)/shard_map/all_gather | solution.py:147
  356.9 181.4 %all-gather.13.cloned.1.call-start = ((), (), s32[]{:S(2)}) async-start(), calls=%async_computation.6 | async-start | bytes 8912896 | tf_op jit(solution)/shard_map/all_gather | solution.py:163
  357.0 87.0 %copy-start.19 = (f32[4096]{0:T(1024)S(1)}, f32[4096]{0:T(1024)}, u32[]{:S(2)}) copy-start(f32[4096]{0:T(1024)} %param.25) | copy-start | bytes 49156
  439.9 5.8 copy-start.5
  459.9 158.0 %all-gather.15.cloned.1.call-start = ((), (), s32[]{:S(2)}) async-start(), calls=%async_computation.8 | async-start | bytes 8912896 | tf_op jit(solution)/shard_map/all_gather | solution.py:164
  462.1 297.7 %reduce-scatter.5.cloned.1.call-start = ((), (), s32[]{:S(2)}) async-start(), calls=%async_computation.7 | async-start | bytes 5242880 | tf_op jit(solution)/shard_map/reduce_scatter | solution.py:222
  712.1 47.6 %copy-start.1 = (f32[128,4096]{1,0:T(8,128)S(1)}, f32[128,4096]{1,0:T(8,128)}, u32[]{:S(2)}) copy-start(f32[128,4096]{1,0:T(8,128)} %convert_add_fusion.1) | copy-start | bytes 6291460
  (3 other events, 3.6 us)
Sparse Core Ops, SparseCore 0:
  10.6 51.6 all-gather.6
  78.2 93.9 all-gather.8
  272.7 80.9 reduce-scatter.2
  357.0 82.8 all-gather.10
  460.0 78.1 all-gather.12
  540.2 77.6 all-gather.14
  712.3 47.4 reduce-scatter.4
where the time goes:
time: 775 us; the launch traced here: 770 us
  waiting for transfers between devices  418 us (54%)
  local copies, waits for them, and re-layouts  173 us (22%)
  matrix products  111 us (14%)
  other arithmetic  50.2 us (6%)
  between operations  15.3 us (2%)
    all_gather x1, waiting for transfers between devices, body(): stream_all = lax.all_gather(stream_own, 'tensor', axis=0, tiled=True)  82.3 us
    reduce_scatter x1, waiting for transfers between devices, body(): lax.psum_scatter(jnp.dot(hyena_mix, hyena_out, preferred_element_type=jnp...  81.1 us
    all_gather x1, waiting for transfers between devices, body(): value_piece = lax.all_gather(values_flat, 'context', axis=0, tiled=True)  79.6 us
    all_gather x1, waiting for transfers between devices, body(): key_piece = lax.all_gather(keys_flat, 'context', axis=0, tiled=True)  75.8 us
    gather x2, local copies, waits for them, and re-layouts, toeplitz(): jnp.take(long_filter, jnp.clip(tap_lag + filter_len, 0, filter_len - 1),...  61.2 us
    gather x2, local copies, waits for them, and re-layouts, toeplitz(): jnp.take(long_filter, jnp.clip(tap_lag, 0, filter_len - 1), axis=1)  60.3 us
    all_gather x1, waiting for transfers between devices, body(): embedded_all = lax.all_gather(embedded, 'tensor', axis=0, tiled=True)  51.8 us
    reduce_scatter x1, waiting for transfers between devices, body(): lax.psum_scatter(jnp.dot(attended, attn_out, preferred_element_type=jnp.f...  47.6 us
  transfers between devices with their start and end apart: 7, of which 6 were waited for; matrix products, arithmetic and copies ran while one was open for 17% of the time, Pallas kernels for 0%

commit v1 on v0

--- a/solution.py
+++ b/solution.py
@@ -161,7 +161,9 @@
         jnp.zeros((2, block_rows, local_heads, HD), jnp.float32),
     )
     key_piece = lax.all_gather(keys_flat, "context", axis=0, tiled=True)
-    value_piece = lax.all_gather(values_flat, "context", axis=0, tiled=True)
+    value_piece = jnp.concatenate(
+        lax.all_to_all(jnp.stack([values_flat] * lax.axis_size("context")), "context", 0, 0), axis=0
+    )
     piece_len = key_piece.shape[0]
     sub_len = math.gcd(piece_len, 512)
 

time: 775 us -> 901 us (1.16)
  matrix products: 111 us -> 163 us
  local copies, waits for them, and re-layouts: 173 us -> 220 us
  other arithmetic: 50.2 us -> 68.2 us
    all_to_all x0 -> x1, waiting for transfers between devices: none -> 130 us  [body(): lax.all_to_all(jnp.stack([values_flat] * lax.axis_size('context')), 'cont...]
    all_gather x1 -> x0, waiting for transfers between devices: 79.6 us -> none  [body(): value_piece = lax.all_gather(values_flat, 'context', axis=0, tiled=True)]
    all_gather x1, waiting for transfers between devices: 75.8 us -> 26.1 us  [body(): key_piece = lax.all_gather(keys_flat, 'context', axis=0, tiled=True)]
    dynamic_slice x0 -> x32, local copies, waits for them, and re-layouts: none -> 33.4 us  [attend_sub(): lax.dynamic_slice_in_dim(value_piece, sub_index * sub_len, sub_len, 0)]
    dot_general x32, matrix products: 22.4 us -> 52.9 us  [attend_sub(): jnp.einsum('qhk,khd->qhd', weights.astype(jnp.bfloat16), value_block, pre...]
    dot_general x32, matrix products: 18.2 us -> 39.5 us  [attend_sub(): jnp.einsum('qhd,khd->qhk', query_rows, key_block, preferred_element_type=...]
    another operation x48, other arithmetic: 1.31 us -> 18.1 us  [attend_sub(): jnp.stack([entry[field] for entry in outputs])]
    all_to_all x0 -> x1, local copies, waits for them, and re-layouts: none -> 12.5 us  [body(): lax.all_to_all(jnp.stack([values_flat] * lax.axis_size('context')), 'cont...]
  transfers between devices with their start and end apart: 7 -> 7, of which waited for: 6 -> 6; matrix products, arithmetic and copies ran while one was open for 17% -> 16% of each run, Pallas kernels for 0% -> 0%
where the time goes in v1:
time: 901 us; the launch traced here: 895 us
  waiting for transfers between devices  420 us (47%)
  local copies, waits for them, and re-layouts  220 us (24%)
  matrix products  163 us (18%)
  other arithmetic  68.2 us (8%)
  between operations  15.4 us (2%)
    all_to_all x1, waiting for transfers between devices, body(): lax.all_to_all(jnp.stack([values_flat] * lax.axis_size('context')), 'cont...  130 us
    all_gather x1, waiting for transfers between devices, body(): stream_all = lax.all_gather(stream_own, 'tensor', axis=0, tiled=True)  82.3 us
    reduce_scatter x1, waiting for transfers between devices, body(): lax.psum_scatter(jnp.dot(hyena_mix, hyena_out, preferred_element_type=jnp...  81.1 us
    gather x2, local copies, waits for them, and re-layouts, toeplitz(): jnp.take(long_filter, jnp.clip(tap_lag + filter_len, 0, filter_len - 1),...  61.2 us
    gather x2, local copies, waits for them, and re-layouts, toeplitz(): jnp.take(long_filter, jnp.clip(tap_lag, 0, filter_len - 1), axis=1)  60.3 us
    dot_general x32, matrix products, attend_sub(): jnp.einsum('qhk,khd->qhd', weights.astype(jnp.bfloat16), value_block, pre...  52.9 us
    all_gather x1, waiting for transfers between devices, body(): embedded_all = lax.all_gather(embedded, 'tensor', axis=0, tiled=True)  51.8 us
    reduce_scatter x1, waiting for transfers between devices, body(): lax.psum_scatter(jnp.dot(attended, attn_out, preferred_element_type=jnp.f...  48.2 us
  transfers between devices with their start and end apart: 7, of which 6 were waited for; matrix products, arithmetic and copies ran while one was open for 16% of the time, Pallas kernels for 0%

profile of v1, /device:TPU:1, one launch (start us, length us, event | category | flops | bytes accessed | tf_op | source)
XLA Modules:
  0.0 894.7 jit_solution(18353546833112443424)
XLA Ops:
  6.5 3.9 convolution_convert_fusion.1
  10.5 51.8 %all-gather.5.cloned.1.call-done = bf16[512,4096]{1,0:T(8,128)(2,1)} async-done(((bf16[128,4096]{1,0:T(8,128)(2,1)}), bf16[512,4096]{1,0:T(8,128)(2,1)}) %all-gather.5.cloned.1.call-update) | async-done | bytes 4194320 | tf_op jit(solution)/shard_map/all_gather | solution.py:103
  65.8 9.9 %fusion.83 = bf16[3,512,512]{2,1,0:T(8,128)(2,1)S(1)} fusion(bf16[3,4096,512]{2,1,0:T(8,128)(2,1)} %param.20, bf16[512,4096]{1,0:T(8,128)(2,1)S(1)} %copy-done.12, f32[4096]{0:T(1024)S(1)} %copy-done.21, f32[512]{0:T(512)S(1)} %add_rsqrt_fusion.1), kind=kOutput, calls=%fused_computation.128 | convolution fusion | flops 6451625984 | bytes 18368512 | tf_op jit(solution)/shard_map/rd,jdc->jrc/dot_general | solution.py:105
  80.9 54.8 %gather_fusion.1 = f32[16384,32]{1,0:T(8,128)} fusion(f32[32,128]{0,1:T(8,128)S(1)} %copy.106, s32[16384]{0:T(1024)S(1)} %bitcast_clamp_fusion), kind=kCustom, calls=%fused_computation.1.clone | custom fusion | bytes 4259840 | tf_op jit(solution)/shard_map/jit(_take)/gather | solution.py:27
  135.7 6.5 copy.111
  142.2 54.8 %gather_fusion = f32[16384,32]{1,0:T(8,128)} fusion(f32[32,128]{0,1:T(8,128)S(1)} %copy.106, s32[16384]{0:T(1024)S(1)} %bitcast_clamp_fusion.1), kind=kCustom, calls=%fused_computation.clone | custom fusion | bytes 4259840 | tf_op jit(solution)/shard_map/jit(_take)/gather | solution.py:26
  196.9 5.5 copy.107
  206.0 8.8 fusion.38
  233.4 5.0 fusion.69
  247.3 5.2 fusion.71
  257.5 4.6 fusion.89
  265.0 7.8 fusion.121
  272.9 81.1 %reduce-scatter.3.cloned.1.call-done = f32[128,4096]{1,0:T(8,128)} async-done(((f32[512,4096]{1,0:T(8,128)}), f32[128,4096]{1,0:T(8,128)}) %reduce-scatter.3.cloned.1.call-update) | async-done | bytes 2097168 | tf_op jit(solution)/shard_map/reduce_scatter | solution.py:140
  357.8 82.3 %all-gather.9.cloned.1.call-done = f32[512,4096]{1,0:T(8,128)} async-done(((f32[128,4096]{1,0:T(8,128)}), f32[512,4096]{1,0:T(8,128)}) %all-gather.9.cloned.1.call-update) | async-done | bytes 8388624 | tf_op jit(solution)/shard_map/all_gather | solution.py:147
  440.1 4.2 multiply_reduce_fusion
  445.9 11.3 %fusion.77 = f32[3,512,512]{1,2,0:T(8,128)} fusion(bf16[3,4096,512]{2,1,0:T(8,128)(2,1)} %param.26, f32[512,4096]{1,0:T(8,128)S(1)} %copy-done.7, f32[4096]{0:T(1024)S(1)} %copy-done.22, f32[512]{0:T(512)S(1)} %add_rsqrt_fusion), kind=kOutput, calls=%fused_computation.126 | convolution fusion | flops 6448742400 | bytes 24135680 | tf_op jit(solution)/shard_map/rd,jdf->jrf/dot_general | solution.py:149
  461.5 4.1 stack.77
  465.6 6.6 all-to-all-start
  472.5 130.4 %all-to-all-done = bf16[16,512,512]{1,2,0:T(8,128)(2,1)} async-done(((bf16[16,512,512]{1,2,0:T(8,128)(2,1)}), bf16[16,512,512]{1,2,0:T(8,128)(2,1)}, u32[]{:S(2)}, u32[]{:S(2)}) %all-to-all-start) | async-done | bytes 8388640 | tf_op jit(solution)/shard_map/all_to_all | solution.py:165
  602.9 12.5 %copy.122 = bf16[16,512,512]{2,1,0:T(8,128)(2,1)} copy(bf16[16,512,512]{1,2,0:T(8,128)(2,1)} %all-to-all-done) | data formatting | bytes 16777216 | tf_op jit(solution)/shard_map/all_to_all | solution.py:165
  615.4 26.1 %all-gather.11.cloned.1.call-done = bf16[8192,512]{0,1:T(8,128)(2,1)} async-done(((bf16[512,512]{0,1:T(8,128)(2,1)}), bf16[8192,512]{0,1:T(8,128)(2,1)}) %all-gather.11.cloned.1.call-update) | async-done | bytes 8388624 | tf_op jit(solution)/shard_map/all_gather | solution.py:163
  642.6 186.0 %while.20 = (s32[]{:T(128)}, f32[2,256,4]{1,2,0:T(4,128)S(1)}, f32[2,256,4]{1,2,0:T(4,128)S(1)}, f32[2,256,4,128]{1,3,2,0:T(8,128)}, s32[32]{0:T(128)S(1)}, /*in...) while((s32[]{:T(128)}, f32[2,256,4]{1,2,0:T(4,128)S(1)}, ...), condition=%wide.region_10.12_spmd.clone, body=%wide.region_4.11_spmd.clone.sunk | while | flops 551627264 | bytes 38447504 | solution.py:216
  830.2 6.5 convolution_convert_fusion
  836.7 48.2 %reduce-scatter.5.cloned.1.call-done = bf16[128,4096]{1,0:T(8,128)(2,1)} async-done(((bf16[512,4096]{1,0:T(8,128)(2,1)}), bf16[128,4096]{1,0:T(8,128)(2,1)}) %reduce-scatter.5.cloned.1.call-update) | async-done | bytes 1048592 | tf_op jit(solution)/shard_map/reduce_scatter | solution.py:224
  (500 shorter events, 245.8 us)
Async XLA Ops:
  6.5 55.8 %all-gather.5.cloned.1.call-start = ((), (), s32[]{:S(2)}) async-start(), calls=%async_computation.3 | async-start | bytes 5242880 | tf_op jit(solution)/shard_map/all_gather | solution.py:103
  10.5 55.1 %copy-start.21 = (f32[4096]{0:T(1024)S(1)}, f32[4096]{0:T(1024)}, u32[]{:S(2)}) copy-start(f32[4096]{0:T(1024)} %param.19) | copy-start | bytes 49156
  10.5 195.5 %all-gather.7.cloned.1.call-start = ((), (), s32[]{:S(2)}) async-start(), calls=%async_computation.4 | async-start | bytes 14204928 | tf_op jit(solution)/shard_map/all_gather | solution.py:119
  62.4 3.4 copy-start.12
  76.9 3.8 copy-start.19
  76.9 3.9 copy-start.18
  78.1 275.8 %reduce-scatter.3.cloned.1.call-start = ((), (), s32[]{:S(2)}) async-start(), calls=%async_computation.5 | async-start | bytes 10485760 | tf_op jit(solution)/shard_map/reduce_scatter | solution.py:140
  206.0 8.8 copy-start.1
  233.4 5.0 copy-start.16
  247.3 5.2 copy-start.10
  272.8 81.2 %copy-start.6 = (bf16[128,4096]{1,0:T(8,128)(2,1)S(1)}, bf16[128,4096]{1,0:T(8,128)(2,1)}, u32[]{:S(2)}) copy-start(bf16[128,4096]{1,0:T(8,128)(2,1)} %convolution_convert_fusion.1) | copy-start | bytes 3145732
  272.8 167.3 %all-gather.9.cloned.1.call-start = ((), (), s32[]{:S(2)}) async-start(), calls=%async_computation.6 | async-start | bytes 10485760 | tf_op jit(solution)/shard_map/all_gather | solution.py:147
  357.1 284.4 %all-gather.11.cloned.1.call-start = ((), (), s32[]{:S(2)}) async-start(), calls=%async_computation.7 | async-start | bytes 8912896 | tf_op jit(solution)/shard_map/all_gather | solution.py:163
  357.3 87.0 %copy-start.22 = (f32[4096]{0:T(1024)S(1)}, f32[4096]{0:T(1024)}, u32[]{:S(2)}) copy-start(f32[4096]{0:T(1024)} %param.25) | copy-start | bytes 49156
  440.1 5.8 copy-start.7
  465.6 137.3 %all-to-all-start = ((bf16[16,512,512]{1,2,0:T(8,128)(2,1)}), bf16[16,512,512]{1,2,0:T(8,128)(2,1)}, u32[]{:S(2)}, u32[]{:S(2)}) async-start(bf16[16,512,512]{1,2,0:T(8,128)(2,1)} %stack.77), calls=%async_computation.1 | async-start | bytes 16777216 | tf_op jit(solution)/shard_map/all_to_all | solution.py:165
  472.1 412.8 %reduce-scatter.5.cloned.1.call-start = ((), (), s32[]{:S(2)}) async-start(), calls=%async_computation.8 | async-start | bytes 5242880 | tf_op jit(solution)/shard_map/reduce_scatter | solution.py:224
  648.7 2.6 copy-start.13
  660.3 2.6 copy-start.13
  683.5 2.6 copy-start.13
  695.2 2.6 copy-start.13
  718.4 2.6 copy-start.13
  730.0 2.6 copy-start.13
  836.7 48.2 %copy-start.2 = (f32[128,4096]{1,0:T(8,128)S(1)}, f32[128,4096]{1,0:T(8,128)}, u32[]{:S(2)}) copy-start(f32[128,4096]{1,0:T(8,128)} %convert_add_fusion.1) | copy-start | bytes 6291460
  (51 other events, 111.5 us)
Sparse Core Ops, SparseCore 0:
  10.6 51.6 all-gather.4
  78.3 93.9 all-gather.6
  273.0 80.9 reduce-scatter.2
  357.2 82.8 all-gather.8
  460.3 181.1 all-gather.10
  836.8 48.0 reduce-scatter.4
